TPU v7x, 256 devices: a whole 4x4x8 slice. The times are simulated.
256 devices in a mesh: grid: 32 (over x, y, z_lo), orb: 8 (over z_hi, core).
Axes of the slice: x: 4, y: 4, z: 8 (z_hi: 4, z_lo: 2; z = z_hi * 2 + z_lo), core: 2. Of those that a mesh axis runs over, the one named last changes fastest.
Arguments:
- orbitals: float32 [512, 128, 8, 128], P('orb', 'grid'), may hold values from -13 to 13, as said below
- potential: float32 [128, 8, 128], P('grid'), may hold values from -1 to 1
Outputs:
- orthonormal: float32 [512, 128, 8, 128], P('orb', 'grid')
Inputs may be any that keep to these rules, and one draw needn't show every extreme that they name: Trial orbitals, real-valued.
All inputs are finite; a program needn't handle non-finite values.
Results may differ from a plain program's by a relative error of at most 0.0003.
Values sent between devices are 32-bit elements; how exact they have to be, the bound alone decides.
A program may use at most 64 MiB of HBM per device.

v0:
```python
import jax
import jax.numpy as jnp
from jax import lax
from jax.sharding import PartitionSpec as P

lap_weights = (-205.0 / 72.0, 8.0 / 5.0, -1.0 / 5.0, 8.0 / 315.0, -1.0 / 560.0)
lower_edge = 3.0
upper_edge = 11.0


def padded_2(cells, sides, width):
    for axis, dim in sides:
        count = lax.axis_size(axis)
        head = lax.slice_in_dim(cells, 0, width, axis=dim)
        tail = lax.slice_in_dim(cells, cells.shape[dim] - width, cells.shape[dim], axis=dim)
        cells = jnp.concatenate(
            [
                lax.ppermute(tail, axis, [(i, (i + 1) % count) for i in range(count)]),
                cells,
                lax.ppermute(head, axis, [((i + 1) % count, i) for i in range(count)]),
            ],
            axis=dim,
        )
    return cells


def wrap_pad(field, axis_num):
    length = field.shape[axis_num]
    head = lax.slice_in_dim(field, length - 4, length, axis=axis_num)
    tail = lax.slice_in_dim(field, 0, 4, axis=axis_num)
    return jnp.concatenate([head, field, tail], axis=axis_num)


def operate(padded_x, field, potential):
    planes = field.shape[1]
    rows_y = field.shape[2]
    cols_z = field.shape[3]
    padded_yz = wrap_pad(wrap_pad(field, 2), 3)
    laplace = 3.0 * lap_weights[0] * field
    for offset in range(1, 5):
        weight = lap_weights[offset]
        along_x = (
            padded_x[:, 4 + offset : 4 + offset + planes]
            + padded_x[:, 4 - offset : 4 - offset + planes]
        )
        along_y = (
            padded_yz[:, :, 4 + offset : 4 + offset + rows_y, 4 : 4 + cols_z]
            + padded_yz[:, :, 4 - offset : 4 - offset + rows_y, 4 : 4 + cols_z]
        )
        along_z = (
            padded_yz[:, :, 4 : 4 + rows_y, 4 + offset : 4 + offset + cols_z]
            + padded_yz[:, :, 4 : 4 + rows_y, 4 - offset : 4 - offset + cols_z]
        )
        laplace = laplace + weight * (along_x + along_y + along_z)
    return potential[None] * field - 0.5 * laplace


def hamiltonian(field, potential):
    padded = padded_2(field, (("grid", 1),), 4)
    return operate(padded, field, potential)


def filter_with(apply_op, start_field, potential):
    center = 0.5 * (upper_edge + lower_edge)
    half_width = 0.5 * (upper_edge - lower_edge)
    prev_field = start_field
    this_field = (apply_op(start_field, potential) - center * start_field) / half_width
    for degree in range(2):
        next_field = (
            2.0 * (apply_op(this_field, potential) - center * this_field) / half_width - prev_field
        )
        prev_field, this_field = (this_field, next_field)
    return this_field


def per_device(orbitals, potential):
    this_field = filter_with(hamiltonian, orbitals, potential)
    local_orbs = orbitals.shape[0]
    field_shape = this_field.shape
    flat_field = this_field.reshape(local_orbs, -1)
    total_cells = float(flat_field.shape[1] * lax.axis_size("grid"))
    contract = (((1,), (1,)), ((), ()))
    highest = lax.Precision.HIGHEST
    gathered = lax.all_gather(flat_field, "orb", axis=0, tiled=True)
    partial_rows = lax.dot_general(flat_field, gathered, contract, precision=highest)
    summed_rows = lax.psum(partial_rows, "grid")
    margin = lax.all_gather(summed_rows, "orb", axis=0, tiled=True) / total_cells
    factor = jnp.linalg.cholesky(margin)
    identity = jnp.eye(margin.shape[0], dtype=jnp.float32)
    inverse = jax.scipy.linalg.solve_triangular(factor, identity, lower=True)
    first_row = lax.axis_index("orb") * local_orbs
    own_rows = lax.dynamic_slice_in_dim(inverse, first_row, local_orbs, 0)
    rotated = jnp.dot(own_rows, gathered, precision=highest)
    return rotated.reshape(field_shape)


def solution(mesh):
    in_specs = (P("orb", "grid", None, None), P("grid", None, None))
    out_specs = P("orb", "grid", None, None)
    return jax.shard_map(
        per_device, mesh=mesh, in_specs=in_specs, out_specs=out_specs, check_vma=False
    )
```

profile of v0, /device:TPU:1, one launch (start us, length us, event | category | flops | bytes accessed | tf_op | source)
XLA Modules:
  0.0 778.8 jit_solution(14914901883185426809)
XLA Ops:
  17.0 5.1 pad_maximum_fusion
  22.1 13.3 %collective-permute-done.1 = f32[64,4,8,128]{3,2,1,0:T(8,128)S(1)} collective-permute-done((f32[64,4,8,128]{3,2,1,0:T(8,128)}, f32[64,4,8,128]{3,2,1,0:T(8,128)S(1)}, u32[]{:S(2)}, u32[]{:S(2)}) %collective-permute-start.1) | collective-permute-done | bytes 1048608 | tf_op jit(solution)/shard_map/ppermute | solution.py:18
  36.4 18.7 %collective-permute-done = f32[64,4,8,128]{3,2,1,0:T(8,128)S(1)} collective-permute-done((f32[64,4,8,128]{3,2,1,0:T(8,128)}, f32[64,4,8,128]{3,2,1,0:T(8,128)S(1)}, u32[]{:S(2)}, u32[]{:S(2)}) %collective-permute-start) | collective-permute-done | bytes 1048608 | tf_op jit(solution)/shard_map/ppermute | solution.py:20
  56.8 16.4 %broadcast_multiply_fusion.1 = (f32[64,4,8,128]{3,2,1,0:T(8,128)S(1)}, f32[64,4,8,128]{3,2,1,0:T(8,128)}) fusion(f32[64,4,8,128]{3,2,1,0:T(8,128)S(1)} %copy-done, f32[64,4,16,132]{3,2,1,0:T(8,128)} %get-tuple-element.34, f32[64,4,16,132]{3,2,1,0:T(8,128)} %get-tuple-element.33, f32[64,4,4,128]{3,2,1,0:T(4,128)S(1)} %get-tuple-element.43, ...), kind=kLoop, calls=%fused_computation.221 | loop fusion | flops 11272192 | bytes 20987904 | tf_op jit(solution)/shard_map/div | solution.py:67
  84.9 14.2 %collective-permute-done.2 = f32[64,4,8,128]{3,2,1,0:T(8,128)S(1)} collective-permute-done((f32[64,4,8,128]{3,2,1,0:T(8,128)S(1)}, f32[64,4,8,128]{3,2,1,0:T(8,128)S(1)}, u32[]{:S(2)}, u32[]{:S(2)}) %collective-permute-start.2) | collective-permute-done | bytes 1048608 | tf_op jit(solution)/shard_map/ppermute | solution.py:20
  99.0 22.7 %collective-permute-done.3 = f32[64,4,8,128]{3,2,1,0:T(8,128)S(1)} collective-permute-done((f32[64,4,8,128]{3,2,1,0:T(8,128)S(1)}, f32[64,4,8,128]{3,2,1,0:T(8,128)S(1)}, u32[]{:S(2)}, u32[]{:S(2)}) %collective-permute-start.3) | collective-permute-done | bytes 1048608 | tf_op jit(solution)/shard_map/ppermute | solution.py:18
  122.8 18.3 %fusion.33 = f32[64,4,8,128]{3,2,1,0:T(8,128)S(1)} fusion(f32[64,4,8,128]{3,2,1,0:T(8,128)S(1)} %copy-done, f32[64,4,8,128]{3,2,1,0:T(8,128)} %copy-done.13, f32[64,4,8,128]{3,2,1,0:T(8,128)S(1)} %get-tuple-element.21, f32[64,4,8,128]{3,2,1,0:T(8,128)} %copy-done.11, f32[64,4,4,128]{3,2,1,0:T(4,128)} %copy-done.3, f32[64,4,4,128]{3,2,1,0:T(4,128)} %copy-done.2, ...), kind=kLoop, calls=%fused_computation.106 | loop fusion | flops 13107200 | bytes 15745024 | tf_op jit(solution)/shard_map/sub | solution.py:70
  151.4 13.0 %collective-permute-done.4 = f32[64,4,8,128]{3,2,1,0:T(8,128)S(1)} collective-permute-done((f32[64,4,8,128]{3,2,1,0:T(8,128)S(1)}, f32[64,4,8,128]{3,2,1,0:T(8,128)S(1)}, u32[]{:S(2)}, u32[]{:S(2)}) %collective-permute-start.4) | collective-permute-done | bytes 1048608 | tf_op jit(solution)/shard_map/ppermute | solution.py:20
  164.5 23.6 %collective-permute-done.5 = f32[64,4,8,128]{3,2,1,0:T(8,128)S(1)} collective-permute-done((f32[64,4,8,128]{3,2,1,0:T(8,128)S(1)}, f32[64,4,8,128]{3,2,1,0:T(8,128)S(1)}, u32[]{:S(2)}, u32[]{:S(2)}) %collective-permute-start.5) | collective-permute-done | bytes 1048608 | tf_op jit(solution)/shard_map/ppermute | solution.py:18
  189.1 18.1 %fusion.12 = f32[64,4,8,128]{3,2,1,0:T(8,128)S(1)} fusion(f32[64,4,8,128]{3,2,1,0:T(8,128)} %copy-done.14, f32[64,4,8,128]{3,2,1,0:T(8,128)S(1)} %fusion.33, f32[64,4,8,128]{3,2,1,0:T(8,128)} %copy-done.12, f32[64,4,4,128]{3,2,1,0:T(4,128)} %copy-done.5, f32[64,4,4,128]{3,2,1,0:T(4,128)} %copy-done.4, f32[64,4,16,132]{3,2,1,0:T(8,128)} %get-tuple-element.26, ...), kind=kLoop, calls=%fused_computation.85 | loop fusion | flops 13369344 | bytes 14696448 | tf_op jit(solution)/shard_map/sub | solution.py:70
  208.8 80.3 %all-gather.3.cloned.1.call-done = f32[512,4096]{1,0:T(8,128)} async-done(((f32[64,4096]{1,0:T(8,128)}), f32[512,4096]{1,0:T(8,128)}) %all-gather.3.cloned.1.call-update) | async-done | bytes 8388624 | tf_op jit(solution)/shard_map/all_gather | solution.py:84
  289.1 11.3 %fusion.142 = f32[64,512]{1,0:T(8,128)} fusion(f32[512,4096]{1,0:T(8,128)} %all-gather.3.cloned.1.call-done, f32[8,8,32,128]{3,2,1,0:T(8,128)S(1)} %bitcast.61), kind=kOutput, calls=%fused_computation.276 | convolution fusion | flops 1610612736 | bytes 9568256 | tf_op jit(solution)/shard_map/dot_general | solution.py:85
  300.6 276.3 %all-reduce.3.cloned.1.call-done = f32[64,512]{1,0:T(8,128)} async-done(((f32[64,512]{1,0:T(8,128)}), f32[64,512]{1,0:T(8,128)}) %all-reduce.3.cloned.1.call-update) | async-done | bytes 131088 | tf_op jit(solution)/shard_map/psum | solution.py:86
  578.2 41.9 %all-gather.5.cloned.1.call-done = f32[512,512]{1,0:T(8,128)} async-done(((f32[64,512]{1,0:T(8,128)}), f32[512,512]{1,0:T(8,128)}) %all-gather.5.cloned.1.call-update) | async-done | bytes 1048592 | tf_op jit(solution)/shard_map/all_gather | solution.py:87
  622.3 11.7 %cholesky.104 = f32[128,128]{1,0:T(8,128)S(1)} custom-call(f32[128,128]{1,0:T(8,128)S(1)} %cholesky.266), custom_call_target="Cholesky" | custom-call | tf_op jit(solution)/shard_map/jit(cholesky)/cholesky | solution.py:88
  634.2 9.8 %custom-call.31 = f32[1,128,128]{1,2,0:T(8,128)S(1)} custom-call(f32[1,128,128]{2,1,0:T(8,128)S(1)} %get-tuple-element.54), custom_call_target="InvertDiagBlocksLowerTriangular" | custom-call | tf_op jit(solution)/shard_map/jit(cholesky)/cholesky | solution.py:88
  644.7 11.7 %cholesky.217 = f32[128,128]{1,0:T(8,128)S(1)} custom-call(f32[128,128]{1,0:T(8,128)S(1)} %cholesky.270), custom_call_target="Cholesky" | custom-call | tf_op jit(solution)/shard_map/jit(cholesky)/cholesky | solution.py:88
  656.4 10.0 %custom-call.32 = f32[1,128,128]{1,2,0:T(8,128)S(1)} custom-call(f32[1,128,128]{2,1,0:T(8,128)S(1)} %get-tuple-element.51), custom_call_target="InvertDiagBlocksLowerTriangular" | custom-call | tf_op jit(solution)/shard_map/jit(cholesky)/cholesky | solution.py:88
  667.1 12.3 %cholesky.238 = f32[128,128]{1,0:T(8,128)} custom-call(f32[128,128]{1,0:T(8,128)S(1)} %cholesky.275), custom_call_target="Cholesky" | custom-call | tf_op jit(solution)/shard_map/jit(cholesky)/cholesky | solution.py:88
  681.6 11.3 %custom-call.33 = f32[1,128,128]{1,2,0:T(8,128)} custom-call(f32[1,128,128]{2,1,0:T(8,128)} %get-tuple-element.48), custom_call_target="InvertDiagBlocksLowerTriangular" | custom-call | tf_op jit(solution)/shard_map/jit(cholesky)/cholesky | solution.py:88
  694.3 11.9 %cholesky.255 = f32[128,128]{1,0:T(8,128)S(1)} custom-call(f32[128,128]{1,0:T(8,128)S(1)} %convolution_subtract_fusion.5), custom_call_target="Cholesky" | custom-call | tf_op jit(solution)/shard_map/jit(cholesky)/cholesky | solution.py:88
  710.1 9.9 %while.1 = (s32[]{:T(128)}, f32[512,512]{1,0:T(8,128)S(1)}, s32[4,2]{0,1:T(2,128)S(1)}, f32[4,128,128]{2,1,0:T(8,128)}, s32[]{:T(128)}) while((s32[]{:T(128)}, f32[512,512]{1,0:T(8,128)S(1)}, s32[4,2]{0,1:T(2,128)S(1)}, f32[4,128,128]{2,1,0:T(8,128)}, s32[]{:T(128)}) %tuple.38), condition=%wide.while_cond, body=%wide.while_body.sunk | while | flops 2 | bytes 132705 | solution.py:90
  720.0 40.1 %custom-call.34 = f32[4,128,128]{1,2,0:T(8,128)S(1)} custom-call(f32[4,128,128]{2,1,0:T(8,128)} %get-tuple-element.12), custom_call_target="InvertDiagBlocksLowerTriangular" | custom-call | tf_op jit(solution)/shard_map/jit(_solve_triangular)/triangular_solve | solution.py:90
  763.2 7.5 convolution_bitcast_fusion
  (107 shorter events, 62.9 us)
Async XLA Ops:
  6.5 9.2 %copy-start = (f32[64,4,8,128]{3,2,1,0:T(8,128)S(1)}, f32[64,4,8,128]{3,2,1,0:T(8,128)}, u32[]{:S(2)}) copy-start(f32[64,4,8,128]{3,2,1,0:T(8,128)} %param.2) | copy-start | bytes 3145732
  6.5 9.2 %copy-start.15 = (f32[4,8,128]{2,1,0:T(8,128)S(1)}, f32[4,8,128]{2,1,0:T(8,128)}, u32[]{:S(2)}) copy-start(f32[4,8,128]{2,1,0:T(8,128)} %param.3) | copy-start | bytes 49156
  6.5 282.6 %all-gather.3.cloned.1.call-start = ((), (), s32[]{:S(2)}) async-start(), calls=%async_computation | async-start | bytes 9437184 | tf_op jit(solution)/shard_map/all_gather | solution.py:84
  6.5 28.8 %collective-permute-start.1 = (f32[64,4,8,128]{3,2,1,0:T(8,128)}, f32[64,4,8,128]{3,2,1,0:T(8,128)S(1)}, u32[]{:S(2)}, u32[]{:S(2)}) collective-permute-start(f32[64,4,8,128]{3,2,1,0:T(8,128)} %param.2), channel_id=1, source_target_pairs={{0,8},{8,16},{16,24},{24,32},{32,40},{40,48},{48,56},{56,64},{64,7... | collective-permute-start | bytes 3145736 | tf_op jit(solution)/shard_map/ppermute | solution.py:18
  9.0 46.1 %collective-permute-start = (f32[64,4,8,128]{3,2,1,0:T(8,128)}, f32[64,4,8,128]{3,2,1,0:T(8,128)S(1)}, u32[]{:S(2)}, u32[]{:S(2)}) collective-permute-start(f32[64,4,8,128]{3,2,1,0:T(8,128)} %param.2), channel_id=1, source_target_pairs={{8,0},{16,8},{24,16},{32,24},{40,32},{48,40},{56,48},{64,56},{72,6... | collective-permute-start | bytes 3145736 | tf_op jit(solution)/shard_map/ppermute | solution.py:20
  35.4 1.0 copy-start.8
  36.4 18.8 %copy-start.7 = (f32[64,8,8,128]{3,2,1,0:T(8,128)}, f32[64,8,8,128]{3,2,1,0:T(8,128)S(1)}, u32[]{:S(2)}) copy-start(f32[64,8,8,128]{3,2,1,0:T(8,128)S(1)} %get-tuple-element.42) | copy-start | bytes 6291460
  55.2 1.6 copy-start.6
  73.2 25.8 %collective-permute-start.2 = (f32[64,4,8,128]{3,2,1,0:T(8,128)S(1)}, f32[64,4,8,128]{3,2,1,0:T(8,128)S(1)}, u32[]{:S(2)}, u32[]{:S(2)}) collective-permute-start(f32[64,4,8,128]{3,2,1,0:T(8,128)S(1)} %get-tuple-element.21), channel_id=1, source_target_pairs={{8,0},{16,8},{24,16},{32,24},{40,32},{48,40},{56,48},{64,56},{72,6... | collective-permute-start | bytes 3145736 | tf_op jit(solution)/shard_map/ppermute | solution.py:20
  78.1 43.6 %collective-permute-start.3 = (f32[64,4,8,128]{3,2,1,0:T(8,128)S(1)}, f32[64,4,8,128]{3,2,1,0:T(8,128)S(1)}, u32[]{:S(2)}, u32[]{:S(2)}) collective-permute-start(f32[64,4,8,128]{3,2,1,0:T(8,128)S(1)} %get-tuple-element.21), channel_id=1, source_target_pairs={{0,8},{8,16},{16,24},{24,32},{32,40},{40,48},{48,56},{56,64},{64,7... | collective-permute-start | bytes 3145736 | tf_op jit(solution)/shard_map/ppermute | solution.py:18
  78.5 1.3 copy-start.2
  78.5 1.3 copy-start.3
  99.0 22.7 %copy-start.11 = (f32[64,4,8,128]{3,2,1,0:T(8,128)}, f32[64,4,8,128]{3,2,1,0:T(8,128)S(1)}, u32[]{:S(2)}) copy-start(f32[64,4,8,128]{3,2,1,0:T(8,128)S(1)} %collective-permute-done.2) | copy-start | bytes 3145732
  121.7 1.1 copy-start.13
  141.1 23.3 %collective-permute-start.4 = (f32[64,4,8,128]{3,2,1,0:T(8,128)S(1)}, f32[64,4,8,128]{3,2,1,0:T(8,128)S(1)}, u32[]{:S(2)}, u32[]{:S(2)}) collective-permute-start(f32[64,4,8,128]{3,2,1,0:T(8,128)S(1)} %fusion.33), channel_id=1, source_target_pairs={{8,0},{16,8},{24,16},{32,24},{40,32},{48,40},{56,48},{64,56},{72,6... | collective-permute-start | bytes 3145736 | tf_op jit(solution)/shard_map/ppermute | solution.py:20
  144.5 43.5 %collective-permute-start.5 = (f32[64,4,8,128]{3,2,1,0:T(8,128)S(1)}, f32[64,4,8,128]{3,2,1,0:T(8,128)S(1)}, u32[]{:S(2)}, u32[]{:S(2)}) collective-permute-start(f32[64,4,8,128]{3,2,1,0:T(8,128)S(1)} %fusion.33), channel_id=1, source_target_pairs={{0,8},{8,16},{16,24},{24,32},{32,40},{40,48},{48,56},{56,64},{64,7... | collective-permute-start | bytes 3145736 | tf_op jit(solution)/shard_map/ppermute | solution.py:18
  145.1 1.3 copy-start.4
  145.1 1.3 copy-start.5
  146.3 42.8 %copy-start.1 = (f32[64,4,8,128]{3,2,1,0:T(8,128)S(1)}, f32[64,4,8,128]{3,2,1,0:T(8,128)}, u32[]{:S(2)}) copy-start(f32[64,4,8,128]{3,2,1,0:T(8,128)} %get-tuple-element.22) | copy-start | bytes 3145732
  164.5 23.6 %copy-start.12 = (f32[64,4,8,128]{3,2,1,0:T(8,128)}, f32[64,4,8,128]{3,2,1,0:T(8,128)S(1)}, u32[]{:S(2)}) copy-start(f32[64,4,8,128]{3,2,1,0:T(8,128)S(1)} %collective-permute-done.4) | copy-start | bytes 3145732
  188.0 1.1 copy-start.14
  208.8 368.2 %all-reduce.3.cloned.1.call-start = ((), (), s32[]{:S(2)}) async-start(), calls=%async_computation.1 | async-start | bytes 262144 | tf_op jit(solution)/shard_map/psum | solution.py:86
  300.4 319.7 %all-gather.5.cloned.1.call-start = ((), (), s32[]{:S(2)}) async-start(), calls=%async_computation.2 | async-start | bytes 1179648 | tf_op jit(solution)/shard_map/all_gather | solution.py:87
  679.4 81.0 %copy-start.10 = (f32[512,512]{1,0:T(8,128)S(1)}, f32[512,512]{1,0:T(8,128)}, u32[]{:S(2)}) copy-start(f32[512,512]{1,0:T(8,128)} %fusion.114) | copy-start | bytes 3145732
  (1 other events, 1.0 us)
Sparse Core Ops, SparseCore 0:
  208.9 80.1 all-gather.2
  300.5 276.3 all-reduce.2
  579.0 41.0 all-gather.4
where the time goes:
time: 786 us; the launch traced here: 779 us
  waiting for transfers between devices  504 us (64%)
  other arithmetic  193 us (25%)
  matrix products  24.5 us (3%)
  local copies, waits for them, and re-layouts  24.2 us (3%)
  between operations  16.5 us (2%)
  starting transfers between devices  16.3 us (2%)
    psum x1, waiting for transfers between devices, per_device(): summed_rows = lax.psum(partial_rows, 'grid')  276 us
    another operation x14, other arithmetic, per_device(): factor = jnp.linalg.cholesky(margin)  82.3 us
    all_gather x1, waiting for transfers between devices, per_device(): gathered = lax.all_gather(flat_field, 'orb', axis=0, tiled=True)  80.3 us
    ppermute x3, waiting for transfers between devices, padded_2(): lax.ppermute(tail, axis, [(i, (i + 1) % count) for i in range(count)])  59.6 us
    ppermute x3, waiting for transfers between devices, padded_2(): lax.ppermute(head, axis, [((i + 1) % count, i) for i in range(count)])  45.9 us
    all_gather x1, waiting for transfers between devices, per_device(): lax.all_gather(summed_rows, 'orb', axis=0, tiled=True) / total_cells  41.9 us
    another operation x3, other arithmetic, per_device(): inverse = jax.scipy.linalg.solve_triangular(factor, identity, lower=True)  40.3 us
    sub x2, other arithmetic, filter_with(): 2.0 * (apply_op(this_field, potential) - center * this_field) / half_width  36.4 us
  transfers between devices with their start and end apart: 9, of which 9 were waited for; matrix products, arithmetic and copies ran while one was open for 3% of the time, Pallas kernels for 0%

commit v1 on v0

--- a/solution.py
+++ b/solution.py
@@ -81,7 +81,9 @@
     total_cells = float(flat_field.shape[1] * lax.axis_size("grid"))
     contract = (((1,), (1,)), ((), ()))
     highest = lax.Precision.HIGHEST
-    gathered = lax.all_gather(flat_field, "orb", axis=0, tiled=True)
+    gathered = jnp.concatenate(
+        lax.all_to_all(jnp.stack([flat_field] * lax.axis_size("orb")), "orb", 0, 0), axis=0
+    )
     partial_rows = lax.dot_general(flat_field, gathered, contract, precision=highest)
     summed_rows = lax.psum(partial_rows, "grid")
     margin = lax.all_gather(summed_rows, "orb", axis=0, tiled=True) / total_cells

time: 786 us -> 895 us (1.14)
  blocking collectives: 0 us -> 198 us
  waiting for transfers between devices: 504 us -> 401 us
  local copies, waits for them, and re-layouts: 24.2 us -> 37.6 us
    all_to_all x0 -> x1, blocking collectives: none -> 198 us  [per_device(): lax.all_to_all(jnp.stack([flat_field] * lax.axis_size('orb')), 'orb', 0, 0)]
    all_gather x1 -> x0, waiting for transfers between devices: 80.3 us -> none  [per_device(): gathered = lax.all_gather(flat_field, 'orb', axis=0, tiled=True)]
    psum x1, waiting for transfers between devices: 276 us -> 263 us  [per_device(): summed_rows = lax.psum(partial_rows, 'grid')]
    dot_general x0 -> x2, local copies, waits for them, and re-layouts: none -> 10.8 us  [per_device(): rotated = jnp.dot(own_rows, gathered, precision=highest)]
    all_gather x1, waiting for transfers between devices: 41.9 us -> 32.7 us  [per_device(): lax.all_gather(summed_rows, 'orb', axis=0, tiled=True) / total_cells]
  transfers between devices with their start and end apart: 9 -> 8, of which waited for: 9 -> 8; matrix products, arithmetic and copies ran while one was open for 3% -> 4% of each run, Pallas kernels for 0% -> 0%
where the time goes in v1:
time: 895 us; the launch traced here: 888 us
  waiting for transfers between devices  401 us (45%)
  blocking collectives  198 us (22%)
  other arithmetic  193 us (22%)
  local copies, waits for them, and re-layouts  37.6 us (4%)
  matrix products  24.7 us (3%)
  between operations  16.9 us (2%)
  starting transfers between devices  15.9 us (2%)
    psum x1, waiting for transfers between devices, per_device(): summed_rows = lax.psum(partial_rows, 'grid')  263 us
    all_to_all x1, blocking collectives, per_device(): lax.all_to_all(jnp.stack([flat_field] * lax.axis_size('orb')), 'orb', 0, 0)  198 us
    another operation x14, other arithmetic, per_device(): factor = jnp.linalg.cholesky(margin)  82.5 us
    ppermute x3, waiting for transfers between devices, padded_2(): lax.ppermute(tail, axis, [(i, (i + 1) % count) for i in range(count)])  59.8 us
    ppermute x3, waiting for transfers between devices, padded_2(): lax.ppermute(head, axis, [((i + 1) % count, i) for i in range(count)])  46.1 us
    another operation x3, other arithmetic, per_device(): inverse = jax.scipy.linalg.solve_triangular(factor, identity, lower=True)  40.3 us
    sub x2, other arithmetic, filter_with(): 2.0 * (apply_op(this_field, potential) - center * this_field) / half_width  36.4 us
    all_gather x1, waiting for transfers between devices, per_device(): lax.all_gather(summed_rows, 'orb', axis=0, tiled=True) / total_cells  32.7 us
  transfers between devices with their start and end apart: 8, of which 8 were waited for; matrix products, arithmetic and copies ran while one was open for 4% of the time, Pallas kernels for 0%

profile of v1, /device:TPU:1, one launch (start us, length us, event | category | flops | bytes accessed | tf_op | source)
XLA Modules:
  0.0 887.8 jit_solution(7418427845406955706)
XLA Ops:
  21.9 13.5 %collective-permute-done.1 = f32[64,4,8,128]{3,2,1,0:T(8,128)S(1)} collective-permute-done((f32[64,4,8,128]{3,2,1,0:T(8,128)}, f32[64,4,8,128]{3,2,1,0:T(8,128)S(1)}, u32[]{:S(2)}, u32[]{:S(2)}) %collective-permute-start.1) | collective-permute-done | bytes 1048608 | tf_op jit(solution)/shard_map/ppermute | solution.py:18
  36.4 18.7 %collective-permute-done = f32[64,4,8,128]{3,2,1,0:T(8,128)S(1)} collective-permute-done((f32[64,4,8,128]{3,2,1,0:T(8,128)}, f32[64,4,8,128]{3,2,1,0:T(8,128)S(1)}, u32[]{:S(2)}, u32[]{:S(2)}) %collective-permute-start) | collective-permute-done | bytes 1048608 | tf_op jit(solution)/shard_map/ppermute | solution.py:20
  56.8 16.1 %broadcast_multiply_fusion.1 = (f32[64,4,8,128]{3,2,1,0:T(8,128)S(1)}, f32[64,4,8,128]{3,2,1,0:T(8,128)}) fusion(f32[64,4,8,128]{3,2,1,0:T(8,128)S(1)} %copy-done.1, f32[64,4,16,132]{3,2,1,0:T(8,128)} %get-tuple-element.34, f32[64,4,16,132]{3,2,1,0:T(8,128)} %get-tuple-element.33, f32[64,4,4,128]{3,2,1,0:T(4,128)S(1)} %get-tuple-element.43, ...), kind=kLoop, calls=%fused_computation.220 | loop fusion | flops 11272192 | bytes 20987904 | tf_op jit(solution)/shard_map/div | solution.py:67
  84.5 14.2 %collective-permute-done.2 = f32[64,4,8,128]{3,2,1,0:T(8,128)S(1)} collective-permute-done((f32[64,4,8,128]{3,2,1,0:T(8,128)S(1)}, f32[64,4,8,128]{3,2,1,0:T(8,128)S(1)}, u32[]{:S(2)}, u32[]{:S(2)}) %collective-permute-start.2) | collective-permute-done | bytes 1048608 | tf_op jit(solution)/shard_map/ppermute | solution.py:20
  98.7 22.7 %collective-permute-done.3 = f32[64,4,8,128]{3,2,1,0:T(8,128)S(1)} collective-permute-done((f32[64,4,8,128]{3,2,1,0:T(8,128)S(1)}, f32[64,4,8,128]{3,2,1,0:T(8,128)S(1)}, u32[]{:S(2)}, u32[]{:S(2)}) %collective-permute-start.3) | collective-permute-done | bytes 1048608 | tf_op jit(solution)/shard_map/ppermute | solution.py:18
  122.5 18.3 %fusion.33 = f32[64,4,8,128]{3,2,1,0:T(8,128)S(1)} fusion(f32[64,4,8,128]{3,2,1,0:T(8,128)S(1)} %copy-done.1, f32[64,4,8,128]{3,2,1,0:T(8,128)} %copy-done.14, f32[64,4,8,128]{3,2,1,0:T(8,128)S(1)} %get-tuple-element.21, f32[64,4,8,128]{3,2,1,0:T(8,128)} %copy-done.12, f32[64,4,4,128]{3,2,1,0:T(4,128)} %copy-done.4, f32[64,4,4,128]{3,2,1,0:T(4,128)} %copy-done.3, ...), kind=kLoop, calls=%fused_computation.105 | loop fusion | flops 13107200 | bytes 15745024 | tf_op jit(solution)/shard_map/sub | solution.py:70
  151.0 13.2 %collective-permute-done.4 = f32[64,4,8,128]{3,2,1,0:T(8,128)S(1)} collective-permute-done((f32[64,4,8,128]{3,2,1,0:T(8,128)S(1)}, f32[64,4,8,128]{3,2,1,0:T(8,128)S(1)}, u32[]{:S(2)}, u32[]{:S(2)}) %collective-permute-start.4) | collective-permute-done | bytes 1048608 | tf_op jit(solution)/shard_map/ppermute | solution.py:20
  164.2 23.6 %collective-permute-done.5 = f32[64,4,8,128]{3,2,1,0:T(8,128)S(1)} collective-permute-done((f32[64,4,8,128]{3,2,1,0:T(8,128)S(1)}, f32[64,4,8,128]{3,2,1,0:T(8,128)S(1)}, u32[]{:S(2)}, u32[]{:S(2)}) %collective-permute-start.5) | collective-permute-done | bytes 1048608 | tf_op jit(solution)/shard_map/ppermute | solution.py:18
  188.8 18.1 %fusion.12 = f32[64,4,8,128]{3,2,1,0:T(8,128)S(1)} fusion(f32[64,4,8,128]{3,2,1,0:T(8,128)} %copy-done.15, f32[64,4,8,128]{3,2,1,0:T(8,128)S(1)} %fusion.33, f32[64,4,8,128]{3,2,1,0:T(8,128)} %copy-done.13, f32[64,4,4,128]{3,2,1,0:T(4,128)} %copy-done.6, f32[64,4,4,128]{3,2,1,0:T(4,128)} %copy-done.5, f32[64,4,16,132]{3,2,1,0:T(8,128)} %get-tuple-element.26, ...), kind=kLoop, calls=%fused_computation.84 | loop fusion | flops 13369344 | bytes 14696448 | tf_op jit(solution)/shard_map/sub | solution.py:70
  208.5 198.1 %all_to_all.5 = f32[8,64,4096]{2,1,0:T(8,128)S(1)} all-to-all(f32[8,64,4096]{2,1,0:T(8,128)S(1)} %stack.3), channel_id=1, replica_groups=mesh['grid'=32,'orb'=8] {'orb'}, dimensions={0} | all-to-all | bytes 16777216 | tf_op jit(solution)/shard_map/all_to_all | solution.py:85
  409.8 8.6 fusion.144
  418.5 262.8 %all-reduce.3.cloned.1.call-done = f32[64,512]{1,0:T(8,128)} async-done(((f32[64,512]{1,0:T(8,128)}), f32[64,512]{1,0:T(8,128)}) %all-reduce.3.cloned.1.call-update) | async-done | bytes 131088 | tf_op jit(solution)/shard_map/psum | solution.py:88
  682.6 9.2 %copy.13 = f32[4096,512]{1,0:T(8,128)} copy(f32[4096,512]{0,1:T(8,128)} %bitcast.66) | data formatting | bytes 16777216 | tf_op jit(solution)/shard_map/dot_general | solution.py:95
  691.7 32.7 %all-gather.2.cloned.1.call-done = f32[512,512]{1,0:T(8,128)} async-done(((f32[64,512]{1,0:T(8,128)}), f32[512,512]{1,0:T(8,128)}) %all-gather.2.cloned.1.call-update) | async-done | bytes 1048592 | tf_op jit(solution)/shard_map/all_gather | solution.py:89
  726.7 11.7 %cholesky.104 = f32[128,128]{1,0:T(8,128)S(1)} custom-call(f32[128,128]{1,0:T(8,128)S(1)} %cholesky.266), custom_call_target="Cholesky" | custom-call | tf_op jit(solution)/shard_map/jit(cholesky)/cholesky | solution.py:90
  738.5 9.8 %custom-call.31 = f32[1,128,128]{1,2,0:T(8,128)S(1)} custom-call(f32[1,128,128]{2,1,0:T(8,128)S(1)} %get-tuple-element.54), custom_call_target="InvertDiagBlocksLowerTriangular" | custom-call | tf_op jit(solution)/shard_map/jit(cholesky)/cholesky | solution.py:90
  749.0 11.7 %cholesky.217 = f32[128,128]{1,0:T(8,128)S(1)} custom-call(f32[128,128]{1,0:T(8,128)S(1)} %cholesky.270), custom_call_target="Cholesky" | custom-call | tf_op jit(solution)/shard_map/jit(cholesky)/cholesky | solution.py:90
  760.8 10.0 %custom-call.32 = f32[1,128,128]{1,2,0:T(8,128)S(1)} custom-call(f32[1,128,128]{2,1,0:T(8,128)S(1)} %get-tuple-element.51), custom_call_target="InvertDiagBlocksLowerTriangular" | custom-call | tf_op jit(solution)/shard_map/jit(cholesky)/cholesky | solution.py:90
  771.5 12.3 %cholesky.238 = f32[128,128]{1,0:T(8,128)} custom-call(f32[128,128]{1,0:T(8,128)S(1)} %cholesky.275), custom_call_target="Cholesky" | custom-call | tf_op jit(solution)/shard_map/jit(cholesky)/cholesky | solution.py:90
  786.1 11.3 %custom-call.33 = f32[1,128,128]{1,2,0:T(8,128)} custom-call(f32[1,128,128]{2,1,0:T(8,128)} %get-tuple-element.48), custom_call_target="InvertDiagBlocksLowerTriangular" | custom-call | tf_op jit(solution)/shard_map/jit(cholesky)/cholesky | solution.py:90
  798.8 11.9 %cholesky.255 = f32[128,128]{1,0:T(8,128)S(1)} custom-call(f32[128,128]{1,0:T(8,128)S(1)} %convolution_subtract_fusion.5), custom_call_target="Cholesky" | custom-call | tf_op jit(solution)/shard_map/jit(cholesky)/cholesky | solution.py:90
  814.8 10.6 %while.1 = (s32[]{:T(128)}, f32[512,512]{1,0:T(8,128)S(1)}, s32[4,2]{0,1:T(2,128)S(1)}, f32[4,128,128]{2,1,0:T(8,128)}, s32[]{:T(128)}) while((s32[]{:T(128)}, f32[512,512]{1,0:T(8,128)S(1)}, s32[4,2]{0,1:T(2,128)S(1)}, f32[4,128,128]{2,1,0:T(8,128)}, s32[]{:T(128)}) %tuple.38), condition=%wide.while_cond, body=%wide.while_body.sunk | while | flops 2 | bytes 132705 | solution.py:92
  825.4 40.1 %custom-call.34 = f32[4,128,128]{1,2,0:T(8,128)S(1)} custom-call(f32[4,128,128]{2,1,0:T(8,128)} %get-tuple-element.12), custom_call_target="InvertDiagBlocksLowerTriangular" | custom-call | tf_op jit(solution)/shard_map/jit(_solve_triangular)/triangular_solve | solution.py:92
  868.6 10.4 %fusion.126 = f32[64,4,8,128]{3,0,2,1:T(8,128)S(1)} fusion(f32[4,8,128,512]{3,2,1,0:T(8,128)} %bitcast.67, s32[]{:T(128)S(6)} %select_n.8, f32[128,512]{1,0:T(8,128)S(1)} %fusion.116, f32[128,512]{1,0:T(8,128)S(1)} %fusion.134, f32[128,512]{1,0:T(8,128)S(1)} %fusion.132, f32[128,512]{1,0:T(8,128)S(1)} %fusion.131), kind=kOutput, calls=%fused_computation.233 | convolution fusion | flops 1610711040 | bytes 10485764 | tf_op jit(solution)/shard_map/dot_general | solution.py:95
  (109 shorter events, 71.9 us)
Async XLA Ops:
  6.5 9.0 %copy-start.1 = (f32[64,4,8,128]{3,2,1,0:T(8,128)S(1)}, f32[64,4,8,128]{3,2,1,0:T(8,128)}, u32[]{:S(2)}) copy-start(f32[64,4,8,128]{3,2,1,0:T(8,128)} %param.2) | copy-start | bytes 3145732
  6.5 9.0 %copy-start.16 = (f32[4,8,128]{2,1,0:T(8,128)S(1)}, f32[4,8,128]{2,1,0:T(8,128)}, u32[]{:S(2)}) copy-start(f32[4,8,128]{2,1,0:T(8,128)} %param.3) | copy-start | bytes 49156
  6.5 674.8 %all-reduce.3.cloned.1.call-start = ((), (), s32[]{:S(2)}) async-start(), calls=%async_computation.1 | async-start | bytes 262144 | tf_op jit(solution)/shard_map/psum | solution.py:88
  6.5 28.8 %collective-permute-start.1 = (f32[64,4,8,128]{3,2,1,0:T(8,128)}, f32[64,4,8,128]{3,2,1,0:T(8,128)S(1)}, u32[]{:S(2)}, u32[]{:S(2)}) collective-permute-start(f32[64,4,8,128]{3,2,1,0:T(8,128)} %param.2), channel_id=1, source_target_pairs={{0,8},{8,16},{16,24},{24,32},{32,40},{40,48},{48,56},{56,64},{64,7... | collective-permute-start | bytes 3145736 | tf_op jit(solution)/shard_map/ppermute | solution.py:18
  9.0 46.1 %collective-permute-start = (f32[64,4,8,128]{3,2,1,0:T(8,128)}, f32[64,4,8,128]{3,2,1,0:T(8,128)S(1)}, u32[]{:S(2)}, u32[]{:S(2)}) collective-permute-start(f32[64,4,8,128]{3,2,1,0:T(8,128)} %param.2), channel_id=1, source_target_pairs={{8,0},{16,8},{24,16},{32,24},{40,32},{48,40},{56,48},{64,56},{72,6... | collective-permute-start | bytes 3145736 | tf_op jit(solution)/shard_map/ppermute | solution.py:20
  35.4 1.0 copy-start.9
  36.4 18.8 %copy-start.8 = (f32[64,8,8,128]{3,2,1,0:T(8,128)}, f32[64,8,8,128]{3,2,1,0:T(8,128)S(1)}, u32[]{:S(2)}) copy-start(f32[64,8,8,128]{3,2,1,0:T(8,128)S(1)} %get-tuple-element.42) | copy-start | bytes 6291460
  55.2 1.6 copy-start.7
  72.9 25.8 %collective-permute-start.2 = (f32[64,4,8,128]{3,2,1,0:T(8,128)S(1)}, f32[64,4,8,128]{3,2,1,0:T(8,128)S(1)}, u32[]{:S(2)}, u32[]{:S(2)}) collective-permute-start(f32[64,4,8,128]{3,2,1,0:T(8,128)S(1)} %get-tuple-element.21), channel_id=1, source_target_pairs={{8,0},{16,8},{24,16},{32,24},{40,32},{48,40},{56,48},{64,56},{72,6... | collective-permute-start | bytes 3145736 | tf_op jit(solution)/shard_map/ppermute | solution.py:20
  77.8 43.6 %collective-permute-start.3 = (f32[64,4,8,128]{3,2,1,0:T(8,128)S(1)}, f32[64,4,8,128]{3,2,1,0:T(8,128)S(1)}, u32[]{:S(2)}, u32[]{:S(2)}) collective-permute-start(f32[64,4,8,128]{3,2,1,0:T(8,128)S(1)} %get-tuple-element.21), channel_id=1, source_target_pairs={{0,8},{8,16},{16,24},{24,32},{32,40},{40,48},{48,56},{56,64},{64,7... | collective-permute-start | bytes 3145736 | tf_op jit(solution)/shard_map/ppermute | solution.py:18
  78.2 1.3 copy-start.3
  78.2 1.3 copy-start.4
  98.7 22.7 %copy-start.12 = (f32[64,4,8,128]{3,2,1,0:T(8,128)}, f32[64,4,8,128]{3,2,1,0:T(8,128)S(1)}, u32[]{:S(2)}) copy-start(f32[64,4,8,128]{3,2,1,0:T(8,128)S(1)} %collective-permute-done.2) | copy-start | bytes 3145732
  121.4 1.1 copy-start.14
  140.8 23.3 %collective-permute-start.4 = (f32[64,4,8,128]{3,2,1,0:T(8,128)S(1)}, f32[64,4,8,128]{3,2,1,0:T(8,128)S(1)}, u32[]{:S(2)}, u32[]{:S(2)}) collective-permute-start(f32[64,4,8,128]{3,2,1,0:T(8,128)S(1)} %fusion.33), channel_id=1, source_target_pairs={{8,0},{16,8},{24,16},{32,24},{40,32},{48,40},{56,48},{64,56},{72,6... | collective-permute-start | bytes 3145736 | tf_op jit(solution)/shard_map/ppermute | solution.py:20
  144.2 43.5 %collective-permute-start.5 = (f32[64,4,8,128]{3,2,1,0:T(8,128)S(1)}, f32[64,4,8,128]{3,2,1,0:T(8,128)S(1)}, u32[]{:S(2)}, u32[]{:S(2)}) collective-permute-start(f32[64,4,8,128]{3,2,1,0:T(8,128)S(1)} %fusion.33), channel_id=1, source_target_pairs={{0,8},{8,16},{16,24},{24,32},{32,40},{40,48},{48,56},{56,64},{64,7... | collective-permute-start | bytes 3145736 | tf_op jit(solution)/shard_map/ppermute | solution.py:18
  144.6 1.3 copy-start.5
  144.6 1.3 copy-start.6
  145.9 42.9 %copy-start.2 = (f32[64,4,8,128]{3,2,1,0:T(8,128)S(1)}, f32[64,4,8,128]{3,2,1,0:T(8,128)}, u32[]{:S(2)}) copy-start(f32[64,4,8,128]{3,2,1,0:T(8,128)} %get-tuple-element.22) | copy-start | bytes 3145732
  164.2 23.6 %copy-start.13 = (f32[64,4,8,128]{3,2,1,0:T(8,128)}, f32[64,4,8,128]{3,2,1,0:T(8,128)S(1)}, u32[]{:S(2)}) copy-start(f32[64,4,8,128]{3,2,1,0:T(8,128)S(1)} %collective-permute-done.4) | copy-start | bytes 3145732
  187.7 1.1 copy-start.15
  406.6 3.2 copy-start
  418.5 305.9 %all-gather.2.cloned.1.call-start = ((), (), s32[]{:S(2)}) async-start(), calls=%async_computation.2 | async-start | bytes 1179648 | tf_op jit(solution)/shard_map/all_gather | solution.py:89
  783.8 82.0 %copy-start.11 = (f32[512,512]{1,0:T(8,128)S(1)}, f32[512,512]{1,0:T(8,128)}, u32[]{:S(2)}) copy-start(f32[512,512]{1,0:T(8,128)} %fusion.114) | copy-start | bytes 3145732
  (1 other events, 1.0 us)
Sparse Core Ops, SparseCore 0:
  418.6 262.6 all-reduce.2
  683.3 41.0 all-gather.1
